TPU v7x, 32 devices: a whole 2x2x4 slice. The times are simulated.
32 devices in a mesh: groups: 2 (over y), locus: 4 (over z), design: 2 (over x), chan: 2 (over core).
Axes of the slice: x: 2, y: 2, z: 4, core: 2. Of those that a mesh axis runs over, the one named last changes fastest.
Arguments:
- base_seq: bfloat16 [4, 2048, 128], P(('groups', 'design'), 'locus'), parts along dimension 0, may hold values from -6 to 6
- deltas: bfloat16 [2048, 512], P(('groups', 'locus', 'design')), parts along dimension 0, may hold values from -6 to 6
- owners: int32 [2048, 1], P(('groups', 'locus', 'design')), parts along dimension 0, may hold values from 0 to 7; in each aligned block of 128 rows (0 to 127, 128 to 255, ...) at most 32 rows name the same one
- slot_ids: int32 [2048], P(('groups', 'locus', 'design')), parts along dimension 0, may hold values from 0 to 127
- stem_weight: bfloat16 [128, 1536], P(None, 'chan'), may hold values from -0.5 to 0.5
- dilated_tap_weight: bfloat16 [3, 1536, 768], P(None, None, 'chan'), may hold values from -0.09375 to 0.09375
- mix_weight: bfloat16 [768, 1536], P('chan'), may hold values from -0.21875 to 0.21875
- head_weight: bfloat16 [1536], replicated, may hold values from -5 to 5
Outputs:
- window_grad: float32 [2048, 512], P(('groups', 'locus', 'design')), parts along dimension 0
There are 2 independent parts, one for each index of `groups`. A program takes and returns all parts, laid end to end along the dimension named above; an argument that names none is the same for every part. Nothing has to cross between parts.
Inputs may be any that keep to these rules, and one draw needn't show every extreme that they name: `owners`: owner o stands for bins of segment o // 2 of locus o % 2. Among the 128 windows of one device no owner is named more than 32 times, a bound that some block reaches. `slot_ids`: several windows may name the same target; their changes add.
All inputs are finite; a program needn't handle non-finite values.
Results may differ from a plain program's by a relative error of at most 0.0055.
Values may be sent and summed in bfloat16 or wider, within the bound.
A program may use at most 64 MiB of HBM per device.

v0:
```python
import jax
import jax.numpy as jnp
from jax import lax
from jax.sharding import PartitionSpec as P

DILATION_STEP = 32


def with_halo(cells, sides, width):
    for axis, dim in sides:
        count = lax.axis_size(axis)
        ends = count - 1
        head = lax.slice_in_dim(cells, 0, width, axis=dim)
        tail = lax.slice_in_dim(cells, cells.shape[dim] - width, cells.shape[dim], axis=dim)
        cells = jnp.concatenate(
            [
                lax.ppermute(tail, axis, [(i, (i + 1) % count) for i in range(ends)]),
                cells,
                lax.ppermute(head, axis, [((i + 1) % count, i) for i in range(ends)]),
            ],
            axis=dim,
        )
    return cells


def silu_slope(pre_value):
    sigmoid_value = jax.nn.sigmoid(pre_value)
    return sigmoid_value * (1.0 + pre_value * (1.0 - sigmoid_value))


def gelu_pull(pre_act, cotangent):
    return jax.vjp(lambda argument: jax.nn.gelu(argument, approximate=True), pre_act)[1](cotangent)[
        0
    ]


def stem_back(pulled, weight):
    upper = pulled.astype(jnp.bfloat16)
    lower = (pulled - upper.astype(jnp.float32)).astype(jnp.bfloat16)
    dims = (((1,), (1,)), ((), ()))
    first = lax.dot_general(upper, weight, dims, preferred_element_type=jnp.float32)
    return first + lax.dot_general(lower, weight, dims, preferred_element_type=jnp.float32)


def shards(
    base_seq, deltas, owners, slot_ids, stem_weight, dilated_tap_weight, mix_weight, head_weight
):
    win_dev, row_width = deltas.shape
    bins_per_device, feat_width = (base_seq.shape[1], base_seq.shape[2])
    slots_dev = bins_per_device * feat_width // row_width
    peer_count = lax.axis_size(("locus", "design"))
    capacity = max(2, 2 * win_dev // peer_count)
    bucket_rows = peer_count * capacity
    target_dev = owners[:, 0]
    member = (target_dev[:, None] == jnp.arange(peer_count, dtype=jnp.int32)[None, :]).astype(
        jnp.int32
    )
    earlier = jnp.cumsum(member, axis=0) - member
    bucket_rank = jnp.sum(earlier * member, axis=1)
    position = target_dev * capacity + bucket_rank
    placer = position[None, :] == jnp.arange(bucket_rows, dtype=jnp.int32)[:, None]
    send_rows = jnp.dot(
        placer.astype(jnp.bfloat16), deltas, preferred_element_type=jnp.float32
    ).astype(jnp.bfloat16)
    send_slots = jnp.sum(jnp.where(placer, slot_ids[None, :], 0), axis=1)
    recv_rows, recv_slots = (
        lax.all_to_all(send_rows, ("locus", "design"), split_axis=0, concat_axis=0, tiled=True),
        lax.all_to_all(send_slots, ("locus", "design"), split_axis=0, concat_axis=0, tiled=True),
    )
    chooser = recv_slots[:, None] == jnp.arange(slots_dev, dtype=jnp.int32)[None, :]
    edit_sum = lax.dot_general(
        chooser.astype(jnp.bfloat16),
        recv_rows,
        (((0,), (0,)), ((), ())),
        preferred_element_type=jnp.float32,
    )
    sequence_onehot = (
        base_seq[0].astype(jnp.float32) + edit_sum.reshape(bins_per_device, feat_width)
    ).astype(jnp.bfloat16)
    padded_sequence = with_halo(sequence_onehot, (("locus", 0),), DILATION_STEP)
    stem_full = lax.all_gather(stem_weight, "chan", axis=1, tiled=True)
    gathered_preactivation = jnp.dot(padded_sequence, stem_full, preferred_element_type=jnp.float32)
    hidden_state = jax.nn.gelu(gathered_preactivation, approximate=True).astype(jnp.bfloat16)
    own_width = dilated_tap_weight.shape[2]
    convolved_output = jnp.zeros((bins_per_device, own_width), jnp.float32)
    for filter_tap in range(3):
        convolved_output = convolved_output + jnp.dot(
            hidden_state[filter_tap * DILATION_STEP : filter_tap * DILATION_STEP + bins_per_device],
            dilated_tap_weight[filter_tap],
            preferred_element_type=jnp.float32,
        )
    mix_grad = jnp.dot(mix_weight, head_weight, preferred_element_type=jnp.float32)
    residual_branch = (silu_slope(convolved_output) * mix_grad[None, :]).astype(jnp.bfloat16)
    padded_gradient = with_halo(residual_branch, (("locus", 0),), DILATION_STEP)
    part_sum = jnp.zeros((bins_per_device, stem_full.shape[1]), jnp.float32)
    for filter_tap in range(3):
        lower_boundary = (2 - filter_tap) * DILATION_STEP
        part_sum = part_sum + lax.dot_general(
            padded_gradient[lower_boundary : lower_boundary + bins_per_device],
            dilated_tap_weight[filter_tap],
            (((1,), (1,)), ((), ())),
            preferred_element_type=jnp.float32,
        )
    local_preactivation = gathered_preactivation[DILATION_STEP : DILATION_STEP + bins_per_device]
    summed = lax.psum(part_sum, "chan")
    hidden_grad = head_weight.astype(jnp.float32)[None, :] + summed
    pulled = gelu_pull(local_preactivation, hidden_grad)
    seq_grad = stem_back(pulled, stem_full)
    slot_grad = seq_grad.reshape(slots_dev, row_width)
    back_rows = jnp.dot(chooser.astype(jnp.float32), slot_grad, precision=lax.Precision.HIGHEST)
    returned = lax.all_to_all(
        back_rows, ("locus", "design"), split_axis=0, concat_axis=0, tiled=True
    )
    return lax.dot_general(
        placer.astype(jnp.float32),
        returned,
        (((0,), (0,)), ((), ())),
        precision=lax.Precision.HIGHEST,
    )


def solution(mesh):
    placed = (
        P(("groups", "design"), "locus", None),
        P(("groups", "locus", "design"), None),
        P(("groups", "locus", "design"), None),
        P(("groups", "locus", "design")),
        P(None, "chan"),
        P(None, None, "chan"),
        P("chan", None),
        P(),
    )
    return jax.shard_map(
        shards,
        mesh=mesh,
        in_specs=placed,
        out_specs=P(("groups", "locus", "design"), None),
        check_vma=False,
    )
```

profile of v0, /device:TPU:0, one launch (start us, length us, event | category | flops | bytes accessed | tf_op | source)
XLA Modules:
  0.0 118.4 jit_solution(7377365366886210995)
XLA Ops:
  6.5 0.0 copy-start
  6.5 0.8 fusion.66
  7.4 0.2 reduce_window_sum.11
  7.6 0.8 select_reduce_fusion.1
  8.4 0.7 multiply_add_fusion
  9.1 0.8 select_reduce_fusion
  9.8 0.7 all_to_all.22
  10.5 7.3 %all-to-all-start = ((s32[8,32,1]{1,2,0:T(1,128)}), s32[8,32,1]{1,2,0:T(1,128)S(1)}, u32[]{:S(2)}, u32[]{:S(2)}) async-start(s32[8,32,1]{1,2,0:T(1,128)} %all_to_all.22), calls=%async_computation | async-start | bytes 8192 | tf_op jit(solution)/shard_map/all_to_all | solution.py:68
  17.8 1.8 %convolution_convert_fusion = bf16[256,512]{1,0:T(8,128)(2,1)} fusion(bf16[128,512]{1,0:T(8,128)(2,1)} %param.9, s32[128]{0:T(128)S(1)} %multiply_add_fusion), kind=kOutput, calls=%fused_computation.29 | convolution fusion | flops 33718272 | bytes 393728 | tf_op jit(solution)/shard_map/dot_general | solution.py:62
  19.6 4.6 %all-to-all-done = s32[8,32,1]{1,2,0:T(1,128)S(1)} async-done(((s32[8,32,1]{1,2,0:T(1,128)}), s32[8,32,1]{1,2,0:T(1,128)S(1)}, u32[]{:S(2)}, u32[]{:S(2)}) %all-to-all-start) | async-done | bytes 1056 | tf_op jit(solution)/shard_map/all_to_all | solution.py:68
  24.2 3.4 %all-to-all-start.1 = ((bf16[8,32,512]{2,1,0:T(8,128)(2,1)}), bf16[8,32,512]{2,1,0:T(8,128)(2,1)S(1)}, u32[]{:S(2)}, u32[]{:S(2)}) async-start(bf16[8,32,512]{2,1,0:T(8,128)(2,1)} %bitcast.4), calls=%async_computation.1 | async-start | bytes 524288 | tf_op jit(solution)/shard_map/all_to_all | solution.py:67
  27.6 0.0 all-reduce.2.cloned.1.call-start
  27.7 0.7 reshape.52
  28.4 0.0 copy-done
  28.4 0.5 convolution_reduce_fusion
  28.9 0.5 broadcast.62
  29.4 0.6 reduce.5
  30.1 0.1 eq.73
  30.1 5.7 %all-to-all-done.1 = bf16[8,32,512]{2,1,0:T(8,128)(2,1)S(1)} async-done(((bf16[8,32,512]{2,1,0:T(8,128)(2,1)}), bf16[8,32,512]{2,1,0:T(8,128)(2,1)S(1)}, u32[]{:S(2)}, u32[]{:S(2)}) %all-to-all-start.1) | async-done | bytes 262176 | tf_op jit(solution)/shard_map/all_to_all | solution.py:67
  35.8 0.3 fusion.61
  36.1 0.0 copy-done.3
  36.2 2.0 %collective-permute-start = (bf16[32,128]{1,0:T(8,128)(2,1)S(1)}, bf16[32,128]{1,0:T(8,128)(2,1)S(1)}, u32[]{:S(2)}, u32[]{:S(2)}) collective-permute-start(bf16[32,128]{1,0:T(8,128)(2,1)S(1)} %get-tuple-element.7), channel_id=1, source_target_pairs={{0,4},{4,8},{8,12},{1,5},{5,9},{9,13},{2,6},{6,10},{10,14},{3,7},{... | collective-permute-start | bytes 24584 | tf_op jit(solution)/shard_map/ppermute | solution.py:17
  38.2 1.3 %collective-permute-start.1 = (bf16[32,128]{1,0:T(8,128)(2,1)S(1)}, bf16[32,128]{1,0:T(8,128)(2,1)S(1)}, u32[]{:S(2)}, u32[]{:S(2)}) collective-permute-start(bf16[32,128]{1,0:T(8,128)(2,1)S(1)} %get-tuple-element.8), channel_id=1, source_target_pairs={{4,0},{8,4},{12,8},{5,1},{9,5},{13,9},{6,2},{10,6},{14,10},{7,3},{... | collective-permute-start | bytes 24584 | tf_op jit(solution)/shard_map/ppermute | solution.py:19
  39.5 0.0 copy-done.2
  39.5 2.1 %all_gather.3 = bf16[128,1536]{1,0:T(8,128)(2,1)S(1)} all-gather(bf16[128,768]{1,0:T(8,128)(2,1)S(1)} %copy-done.2), channel_id=1, replica_groups=mesh['groups'=2,'locus'=4,'design'=2,'chan'=2] {'chan'}, dimensions={1}, use_global_device_ids=true | all-gather | bytes 589824 | tf_op jit(solution)/shard_map/all_gather | solution.py:81
  41.6 0.0 collective-permute-done
  41.6 2.1 %collective-permute-done.1 = bf16[32,128]{1,0:T(8,128)(2,1)S(1)} collective-permute-done((bf16[32,128]{1,0:T(8,128)(2,1)S(1)}, bf16[32,128]{1,0:T(8,128)(2,1)S(1)}, u32[]{:S(2)}, u32[]{:S(2)}) %collective-permute-start.1) | collective-permute-done | bytes 8224 | tf_op jit(solution)/shard_map/ppermute | solution.py:19
  43.8 2.9 %fusion.7 = (bf16[576,1536]{1,0:T(8,128)(2,1)S(1)}, f32[576,1536]{1,0:T(8,128)}) fusion(bf16[128,1536]{1,0:T(8,128)(2,1)S(1)} %all_gather.3, bf16[32,128]{1,0:T(8,128)(2,1)S(1)} %collective-permute-done.1, bf16[512,128]{1,0:T(8,128)(2,1)S(1)} %fusion.50, bf16[32,128]{1,0:T(8,128)(2,1)S(1)} %collective-permute-done), kind=kOutput, calls=%fused_computation.10 | convolution fusion | flops 234897408 | bytes 5849088 | tf_op jit(solution)/shard_map/dot_general | solution.py:82
  46.7 0.0 copy-done.1
  46.7 1.0 fusion.18
  47.7 1.0 fusion.22
  48.7 1.2 multiply_convert_fusion
  49.9 2.9 %collective-permute-start.3 = (bf16[32,384]{1,0:T(8,128)(2,1)S(1)}, bf16[32,384]{1,0:T(8,128)(2,1)S(1)}, u32[]{:S(2)}, u32[]{:S(2)}) collective-permute-start(bf16[32,384]{1,0:T(8,128)(2,1)S(1)} %get-tuple-element.6), channel_id=1, source_target_pairs={{0,4},{4,8},{8,12},{1,5},{5,9},{9,13},{2,6},{6,10},{10,14},{3,7},{... | collective-permute-start | bytes 73736 | tf_op jit(solution)/shard_map/ppermute | solution.py:17
  52.8 1.0 fusion.31
  53.8 1.3 %collective-permute-start.2 = (bf16[32,384]{1,0:T(8,128)(2,1)S(1)}, bf16[32,384]{1,0:T(8,128)(2,1)S(1)}, u32[]{:S(2)}, u32[]{:S(2)}) collective-permute-start(bf16[32,384]{1,0:T(8,128)(2,1)S(1)} %get-tuple-element.5), channel_id=1, source_target_pairs={{4,0},{8,4},{12,8},{5,1},{9,5},{13,9},{6,2},{10,6},{14,10},{7,3},{... | collective-permute-start | bytes 73736 | tf_op jit(solution)/shard_map/ppermute | solution.py:19
  55.1 0.0 collective-permute-done.3
  55.1 1.0 fusion.28
  56.1 3.4 %collective-permute-done.2 = bf16[32,384]{1,0:T(8,128)(2,1)S(1)} collective-permute-done((bf16[32,384]{1,0:T(8,128)(2,1)S(1)}, bf16[32,384]{1,0:T(8,128)(2,1)S(1)}, u32[]{:S(2)}, u32[]{:S(2)}) %collective-permute-start.2) | collective-permute-done | bytes 24608 | tf_op jit(solution)/shard_map/ppermute | solution.py:19
  59.5 2.8 %fusion.8 = f32[512,1536]{1,0:T(8,128)} fusion(f32[512,1536]{1,0:T(8,128)S(1)} %fusion.28, f32[512,1536]{1,0:T(8,128)S(1)} %fusion.31, bf16[3,1536,384]{2,1,0:T(8,128)(2,1)S(1)} %copy-done.1, bf16[32,384]{1,0:T(8,128)(2,1)S(1)} %collective-permute-done.2, bf16[512,384]{1,0:T(8,128)(2,1)S(1)} %multiply_convert_fusion), kind=kOutput, calls=%fused_computation.12 | convolution fusion | flops 606339072 | bytes 11034624 | tf_op jit(solution)/shard_map/dot_general | solution.py:98
  62.3 0.0 all-reduce.2.cloned.1.call-update
  62.3 0.7 copy-done.4
  63.0 21.2 %all-reduce.2.cloned.1.call-done = f32[512,1536]{1,0:T(8,128)} async-done(((f32[512,1536]{1,0:T(8,128)}), f32[512,1536]{1,0:T(8,128)}) %all-reduce.2.cloned.1.call-update) | async-done | bytes 3145744 | tf_op jit(solution)/shard_map/psum | solution.py:105
  84.2 4.1 %fusion.14 = f32[512,1536]{1,0:T(8,128)S(1)} fusion(f32[576,1536]{1,0:T(8,128)} %get-tuple-element.10, f32[512,1536]{1,0:T(8,128)} %all-reduce.2.cloned.1.call-done, f32[1536]{0:T(1024)S(1)} %convert_element_type.38), kind=kLoop, calls=%fused_computation.18 | loop fusion | flops 15728640 | bytes 9443328 | tf_op jit(solution)/shard_map/transpose(jvp())/add_any | solution.py:32
  88.3 0.6 fusion.15
  88.9 0.6 convolution_add_fusion.1
  89.5 0.4 fusion.59
  89.9 20.5 %all_to_all.33 = f32[8,32,512]{2,1,0:T(8,128)S(1)} all-to-all(f32[8,32,512]{2,1,0:T(8,128)S(1)} %fusion.59), channel_id=1, replica_groups=mesh['groups'=2,'locus'=4,'design'=2,'chan'=2] {'locus','design'}, dimensions={0} | all-to-all | bytes 1048576 | tf_op jit(solution)/shard_map/all_to_all | solution.py:111
  110.4 1.1 fusion.57
  (10 shorter events, 0.1 us)
Async XLA Ops:
  6.5 21.9 %copy-start = (bf16[384,1536]{1,0:T(8,128)(2,1)S(1)}, bf16[384,1536]{1,0:T(8,128)(2,1)}, u32[]{:S(2)}) copy-start(bf16[384,1536]{1,0:T(8,128)(2,1)} %param.14) | copy-start | bytes 3538948
  6.5 29.6 %copy-start.3 = (bf16[1,512,128]{2,1,0:T(8,128)(2,1)S(1)}, bf16[1,512,128]{2,1,0:T(8,128)(2,1)}, u32[]{:S(2)}) copy-start(bf16[1,512,128]{2,1,0:T(8,128)(2,1)} %param.8) | copy-start | bytes 393220
  6.5 33.0 %copy-start.2 = (bf16[128,768]{1,0:T(8,128)(2,1)S(1)}, bf16[128,768]{1,0:T(8,128)(2,1)}, u32[]{:S(2)}) copy-start(bf16[128,768]{1,0:T(8,128)(2,1)} %param.12) | copy-start | bytes 589828
  10.5 13.7 %all-to-all-start = ((s32[8,32,1]{1,2,0:T(1,128)}), s32[8,32,1]{1,2,0:T(1,128)S(1)}, u32[]{:S(2)}, u32[]{:S(2)}) async-start(s32[8,32,1]{1,2,0:T(1,128)} %all_to_all.22), calls=%async_computation | async-start | bytes 8192 | tf_op jit(solution)/shard_map/all_to_all | solution.py:68
  24.2 11.6 %all-to-all-start.1 = ((bf16[8,32,512]{2,1,0:T(8,128)(2,1)}), bf16[8,32,512]{2,1,0:T(8,128)(2,1)S(1)}, u32[]{:S(2)}, u32[]{:S(2)}) async-start(bf16[8,32,512]{2,1,0:T(8,128)(2,1)} %bitcast.4), calls=%async_computation.1 | async-start | bytes 524288 | tf_op jit(solution)/shard_map/all_to_all | solution.py:67
  27.6 56.6 %all-reduce.2.cloned.1.call-start = ((), (), s32[]{:S(2)}) async-start(), calls=%async_computation.3 | async-start | bytes 6291456 | tf_op jit(solution)/shard_map/psum | solution.py:105
  36.2 5.4 %collective-permute-start = (bf16[32,128]{1,0:T(8,128)(2,1)S(1)}, bf16[32,128]{1,0:T(8,128)(2,1)S(1)}, u32[]{:S(2)}, u32[]{:S(2)}) collective-permute-start(bf16[32,128]{1,0:T(8,128)(2,1)S(1)} %get-tuple-element.7), channel_id=1, source_target_pairs={{0,4},{4,8},{8,12},{1,5},{5,9},{9,13},{2,6},{6,10},{10,14},{3,7},{... | collective-permute-start | bytes 24584 | tf_op jit(solution)/shard_map/ppermute | solution.py:17
  38.2 5.5 %collective-permute-start.1 = (bf16[32,128]{1,0:T(8,128)(2,1)S(1)}, bf16[32,128]{1,0:T(8,128)(2,1)S(1)}, u32[]{:S(2)}, u32[]{:S(2)}) collective-permute-start(bf16[32,128]{1,0:T(8,128)(2,1)S(1)} %get-tuple-element.8), channel_id=1, source_target_pairs={{4,0},{8,4},{12,8},{5,1},{9,5},{13,9},{6,2},{10,6},{14,10},{7,3},{... | collective-permute-start | bytes 24584 | tf_op jit(solution)/shard_map/ppermute | solution.py:19
  41.6 5.1 %copy-start.1 = (bf16[3,1536,384]{2,1,0:T(8,128)(2,1)S(1)}, bf16[3,1536,384]{2,1,0:T(8,128)(2,1)}, u32[]{:S(2)}) copy-start(bf16[3,1536,384]{2,1,0:T(8,128)(2,1)} %param.13) | copy-start | bytes 10616836
  49.9 5.3 %collective-permute-start.3 = (bf16[32,384]{1,0:T(8,128)(2,1)S(1)}, bf16[32,384]{1,0:T(8,128)(2,1)S(1)}, u32[]{:S(2)}, u32[]{:S(2)}) collective-permute-start(bf16[32,384]{1,0:T(8,128)(2,1)S(1)} %get-tuple-element.6), channel_id=1, source_target_pairs={{0,4},{4,8},{8,12},{1,5},{5,9},{9,13},{2,6},{6,10},{10,14},{3,7},{... | collective-permute-start | bytes 73736 | tf_op jit(solution)/shard_map/ppermute | solution.py:17
  53.8 5.7 %collective-permute-start.2 = (bf16[32,384]{1,0:T(8,128)(2,1)S(1)}, bf16[32,384]{1,0:T(8,128)(2,1)S(1)}, u32[]{:S(2)}, u32[]{:S(2)}) collective-permute-start(bf16[32,384]{1,0:T(8,128)(2,1)S(1)} %get-tuple-element.5), channel_id=1, source_target_pairs={{4,0},{8,4},{12,8},{5,1},{9,5},{13,9},{6,2},{10,6},{14,10},{7,3},{... | collective-permute-start | bytes 73736 | tf_op jit(solution)/shard_map/ppermute | solution.py:19
  62.3 0.7 copy-start.4
Sparse Core Ops, SparseCore 0:
  62.4 21.7 all-reduce.1
where the time goes:
time: 119 us; the launch traced here: 118 us
  waiting for transfers between devices  37.1 us (31%)
  blocking collectives  22.6 us (19%)
  starting transfers between devices  18.2 us (15%)
  matrix products  16 us (13%)
  between operations  13.6 us (11%)
  other arithmetic  8.02 us (7%)
  local copies, waits for them, and re-layouts  2.73 us (2%)
    psum x1, waiting for transfers between devices, shards(): summed = lax.psum(part_sum, 'chan')  21.2 us
    all_to_all x1, blocking collectives, shards(): lax.all_to_all(back_rows, ('locus', 'design'), split_axis=0, concat_axis=...  20.5 us
    all_to_all x1, starting transfers between devices, shards(): lax.all_to_all(send_slots, ('locus', 'design'), split_axis=0, concat_axis...  7.25 us
    all_to_all x1, waiting for transfers between devices, shards(): lax.all_to_all(send_rows, ('locus', 'design'), split_axis=0, concat_axis=...  5.68 us
    ppermute x2, waiting for transfers between devices, with_halo(): lax.ppermute(head, axis, [((i + 1) % count, i) for i in range(ends)])  5.54 us
    ppermute x2, starting transfers between devices, with_halo(): lax.ppermute(tail, axis, [(i, (i + 1) % count) for i in range(ends)])  4.95 us
    dot_general x3, matrix products, shards(): lax.dot_general(padded_gradient[lower_boundary:lower_boundary + bins_per_...  4.77 us
    all_to_all x1, waiting for transfers between devices, shards(): lax.all_to_all(send_slots, ('locus', 'design'), split_axis=0, concat_axis...  4.64 us
  transfers between devices with their start and end apart: 7, of which 5 were waited for; matrix products, arithmetic and copies ran while one was open for 5% of the time, Pallas kernels for 0%

commit v1 on v0

--- a/solution.py
+++ b/solution.py
@@ -4,6 +4,23 @@
 from jax.sharding import PartitionSpec as P
 
 DILATION_STEP = 32
+
+
+def _solve_sums_all(frame_in, axis_no, arr):
+    block_now = frame_in.shape
+    return jnp.moveaxis(
+        frame_in.reshape(
+            *block_now[:axis_no], arr, block_now[axis_no] // arr, *block_now[axis_no + 1 :]
+        ),
+        axis_no,
+        0,
+    )
+
+
+def map_the_columns(obj, ndim_at):
+    obj = jnp.moveaxis(obj, 0, ndim_at)
+    heard = obj.shape
+    return obj.reshape(*heard[:ndim_at], heard[ndim_at] * heard[ndim_at + 1], *heard[ndim_at + 2 :])
 
 
 def with_halo(cells, sides, width):
@@ -45,6 +62,19 @@
 def shards(
     base_seq, deltas, owners, slot_ids, stem_weight, dilated_tap_weight, mix_weight, head_weight
 ):
+
+    def pass_domain_now(patch, ax_name, tile_in, sample):
+        low, oldest = (lax.axis_size(ax_name), lax.axis_index(ax_name))
+        e_now = _solve_sums_all(patch, tile_in, low)
+        arrivals = [e_now[oldest]]
+        for c in range(1, low):
+            plain = e_now[(oldest + c) % low]
+            arrivals.append(
+                lax.ppermute(plain, ax_name, [(src_i, (src_i + c) % low) for src_i in range(low)])
+            )
+        e_now = jnp.stack(arrivals)[(oldest - jnp.arange(low)) % low]
+        return map_the_columns(e_now, sample)
+
     win_dev, row_width = deltas.shape
     bins_per_device, feat_width = (base_seq.shape[1], base_seq.shape[2])
     slots_dev = bins_per_device * feat_width // row_width
@@ -64,7 +94,7 @@
     ).astype(jnp.bfloat16)
     send_slots = jnp.sum(jnp.where(placer, slot_ids[None, :], 0), axis=1)
     recv_rows, recv_slots = (
-        lax.all_to_all(send_rows, ("locus", "design"), split_axis=0, concat_axis=0, tiled=True),
+        pass_domain_now(send_rows, ("locus", "design"), 0, 0),
         lax.all_to_all(send_slots, ("locus", "design"), split_axis=0, concat_axis=0, tiled=True),
     )
     chooser = recv_slots[:, None] == jnp.arange(slots_dev, dtype=jnp.int32)[None, :]

time: 119 us -> 127 us (1.067)
  starting transfers between devices: 18.2 us -> 23.2 us
  waiting for transfers between devices: 37.1 us -> 40.2 us
    ppermute x0 -> x7, waiting for transfers between devices: none -> 14.2 us  [pass_domain_now(): lax.ppermute(plain, ax_name, [(src_i, (src_i + c) % low) for src_i in ran...]
    ppermute x0 -> x7, starting transfers between devices: none -> 9.59 us  [pass_domain_now(): lax.ppermute(plain, ax_name, [(src_i, (src_i + c) % low) for src_i in ran...]
    all_to_all x1 -> x0, waiting for transfers between devices: 5.68 us -> none  [shards(): lax.all_to_all(send_rows, ('locus', 'design'), split_axis=0, concat_axis=...]
    all_to_all x1, waiting for transfers between devices: 4.64 us -> 0.01 us  [shards(): lax.all_to_all(send_slots, ('locus', 'design'), split_axis=0, concat_axis...]
    all_to_all x1 -> x0, starting transfers between devices: 3.41 us -> none  [shards(): lax.all_to_all(send_rows, ('locus', 'design'), split_axis=0, concat_axis=...]
  transfers between devices with their start and end apart: 7 -> 13, of which waited for: 5 -> 6; matrix products, arithmetic and copies ran while one was open for 5% -> 4% of each run, Pallas kernels for 0% -> 0%
where the time goes in v1:
time: 127 us; the launch traced here: 126 us
  waiting for transfers between devices  40.2 us (32%)
  starting transfers between devices  23.2 us (18%)
  blocking collectives  22.6 us (18%)
  matrix products  15.3 us (12%)
  between operations  13.8 us (11%)
  other arithmetic  8.05 us (6%)
  local copies, waits for them, and re-layouts  3.34 us (3%)
    all_to_all x1, blocking collectives, shards(): lax.all_to_all(back_rows, ('locus', 'design'), split_axis=0, concat_axis=...  20.5 us
    psum x1, waiting for transfers between devices, shards(): summed = lax.psum(part_sum, 'chan')  20.4 us
    ppermute x7, waiting for transfers between devices, pass_domain_now(): lax.ppermute(plain, ax_name, [(src_i, (src_i + c) % low) for src_i in ran...  14.2 us
    ppermute x7, starting transfers between devices, pass_domain_now(): lax.ppermute(plain, ax_name, [(src_i, (src_i + c) % low) for src_i in ran...  9.59 us
    all_to_all x1, starting transfers between devices, shards(): lax.all_to_all(send_slots, ('locus', 'design'), split_axis=0, concat_axis...  7.25 us
    ppermute x2, waiting for transfers between devices, with_halo(): lax.ppermute(head, axis, [((i + 1) % count, i) for i in range(ends)])  5.54 us
    dot_general x3, matrix products, shards(): lax.dot_general(padded_gradient[lower_boundary:lower_boundary + bins_per_...  4.74 us
    add_any x1, other arithmetic, gelu_pull(): jax.nn.gelu(argument, approximate=True)  4.06 us
  transfers between devices with their start and end apart: 13, of which 6 were waited for; matrix products, arithmetic and copies ran while one was open for 4% of the time, Pallas kernels for 0%

profile of v1, /device:TPU:0, one launch (start us, length us, event | category | flops | bytes accessed | tf_op | source)
XLA Modules:
  0.0 126.5 jit_solution(15950553616746433226)
XLA Ops:
  6.5 0.8 fusion.66
  7.4 0.2 reduce_window_sum.11
  7.6 0.8 select_reduce_fusion.1
  8.4 0.7 multiply_add_fusion
  9.1 0.8 select_reduce_fusion
  9.8 0.7 all_to_all.14
  10.5 7.3 %all-to-all-start = ((s32[8,32,1]{1,2,0:T(1,128)}), s32[8,32,1]{1,2,0:T(1,128)S(1)}, u32[]{:S(2)}, u32[]{:S(2)}) async-start(s32[8,32,1]{1,2,0:T(1,128)} %all_to_all.14), calls=%async_computation | async-start | bytes 8192 | tf_op jit(solution)/shard_map/all_to_all | solution.py:98
  17.8 0.0 all-reduce.2.cloned.1.call-start
  17.9 1.1 convolution_convert_fusion
  19.1 4.6 %collective-permute-start.6 = (bf16[32,512]{1,0:T(8,128)(2,1)S(1)}, bf16[32,512]{1,0:T(8,128)(2,1)S(1)}, u32[]{:S(2)}, u32[]{:S(2)}) collective-permute-start(bf16[32,512]{1,0:T(8,128)(2,1)S(1)} %get-tuple-element.7), channel_id=1, source_target_pairs={{0,14},{2,0},{4,2},{6,4},{8,6},{10,8},{12,10},{14,12},{1,15},{3,1}... | collective-permute-start | bytes 98312 | tf_op jit(solution)/shard_map/ppermute | solution.py:73
  23.8 0.6 collective-permute-start.5
  24.3 2.9 %collective-permute-start.3 = (bf16[32,512]{1,0:T(8,128)(2,1)S(1)}, bf16[32,512]{1,0:T(8,128)(2,1)S(1)}, u32[]{:S(2)}, u32[]{:S(2)}) collective-permute-start(bf16[32,512]{1,0:T(8,128)(2,1)S(1)} %get-tuple-element.10), channel_id=1, source_target_pairs={{0,8},{2,10},{4,12},{6,14},{8,0},{10,2},{12,4},{14,6},{1,9},{3,11}... | collective-permute-start | bytes 98312 | tf_op jit(solution)/shard_map/ppermute | solution.py:73
  27.2 1.5 %collective-permute-start = (bf16[32,512]{1,0:T(8,128)(2,1)S(1)}, bf16[32,512]{1,0:T(8,128)(2,1)S(1)}, u32[]{:S(2)}, u32[]{:S(2)}) collective-permute-start(bf16[32,512]{1,0:T(8,128)(2,1)S(1)} %get-tuple-element.13), channel_id=1, source_target_pairs={{0,2},{2,4},{4,6},{6,8},{8,10},{10,12},{12,14},{14,0},{1,3},{3,5},... | collective-permute-start | bytes 98312 | tf_op jit(solution)/shard_map/ppermute | solution.py:73
  28.7 0.7 reshape.115
  29.4 0.5 convolution_reduce_fusion
  29.9 0.0 all-to-all-done
  29.9 0.5 broadcast.138
  30.4 0.7 reduce.5
  31.1 0.1 eq.83
  31.2 2.8 %collective-permute-done = bf16[32,512]{1,0:T(8,128)(2,1)S(1)} collective-permute-done((bf16[32,512]{1,0:T(8,128)(2,1)S(1)}, bf16[32,512]{1,0:T(8,128)(2,1)S(1)}, u32[]{:S(2)}, u32[]{:S(2)}) %collective-permute-start) | collective-permute-done | bytes 32800 | tf_op jit(solution)/shard_map/ppermute | solution.py:73
  34.0 5.7 %collective-permute-done.1 = bf16[32,512]{1,0:T(8,128)(2,1)S(1)} collective-permute-done((bf16[32,512]{1,0:T(8,128)(2,1)S(1)}, bf16[32,512]{1,0:T(8,128)(2,1)S(1)}, u32[]{:S(2)}, u32[]{:S(2)}) %collective-permute-start.1) | collective-permute-done | bytes 32800 | tf_op jit(solution)/shard_map/ppermute | solution.py:73
  39.7 0.0 collective-permute-start.2
  39.7 5.7 %collective-permute-done.2 = bf16[32,512]{1,0:T(8,128)(2,1)S(1)} collective-permute-done((bf16[32,512]{1,0:T(8,128)(2,1)S(1)}, bf16[32,512]{1,0:T(8,128)(2,1)S(1)}, u32[]{:S(2)}, u32[]{:S(2)}) %collective-permute-start.2) | collective-permute-done | bytes 32800 | tf_op jit(solution)/shard_map/ppermute | solution.py:73
  45.5 0.6 gather_fusion
  46.0 0.3 fusion.61
  46.4 1.3 %collective-permute-start.7 = (bf16[32,128]{1,0:T(8,128)(2,1)S(1)}, bf16[32,128]{1,0:T(8,128)(2,1)S(1)}, u32[]{:S(2)}, u32[]{:S(2)}) collective-permute-start(bf16[32,128]{1,0:T(8,128)(2,1)S(1)} %get-tuple-element.15), channel_id=1, source_target_pairs={{0,4},{4,8},{8,12},{1,5},{5,9},{9,13},{2,6},{6,10},{10,14},{3,7},{... | collective-permute-start | bytes 24584 | tf_op jit(solution)/shard_map/ppermute | solution.py:34
  47.7 1.3 %collective-permute-start.8 = (bf16[32,128]{1,0:T(8,128)(2,1)S(1)}, bf16[32,128]{1,0:T(8,128)(2,1)S(1)}, u32[]{:S(2)}, u32[]{:S(2)}) collective-permute-start(bf16[32,128]{1,0:T(8,128)(2,1)S(1)} %get-tuple-element.16), channel_id=1, source_target_pairs={{4,0},{8,4},{12,8},{5,1},{9,5},{13,9},{6,2},{10,6},{14,10},{7,3},{... | collective-permute-start | bytes 24584 | tf_op jit(solution)/shard_map/ppermute | solution.py:36
  49.0 2.1 %all_gather.3 = bf16[128,1536]{1,0:T(8,128)(2,1)S(1)} all-gather(bf16[128,768]{1,0:T(8,128)(2,1)S(1)} %copy-done.2), channel_id=1, replica_groups=mesh['groups'=2,'locus'=4,'design'=2,'chan'=2] {'chan'}, dimensions={1}, use_global_device_ids=true | all-gather | bytes 589824 | tf_op jit(solution)/shard_map/all_gather | solution.py:111
  51.1 2.1 %collective-permute-done.8 = bf16[32,128]{1,0:T(8,128)(2,1)S(1)} collective-permute-done((bf16[32,128]{1,0:T(8,128)(2,1)S(1)}, bf16[32,128]{1,0:T(8,128)(2,1)S(1)}, u32[]{:S(2)}, u32[]{:S(2)}) %collective-permute-start.8) | collective-permute-done | bytes 8224 | tf_op jit(solution)/shard_map/ppermute | solution.py:36
  53.3 2.9 %fusion.7 = (bf16[576,1536]{1,0:T(8,128)(2,1)S(1)}, f32[576,1536]{1,0:T(8,128)}) fusion(bf16[128,1536]{1,0:T(8,128)(2,1)S(1)} %all_gather.3, bf16[32,128]{1,0:T(8,128)(2,1)S(1)} %collective-permute-done.8, bf16[512,128]{1,0:T(8,128)(2,1)S(1)} %fusion.50, bf16[32,128]{1,0:T(8,128)(2,1)S(1)} %collective-permute-done.7), kind=kOutput, calls=%fused_computation.11 | convolution fusion | flops 234897408 | bytes 5849088 | tf_op jit(solution)/shard_map/dot_general | solution.py:112
  56.2 1.0 fusion.18
  57.2 1.0 fusion.22
  58.2 1.2 multiply_convert_fusion
  59.4 2.4 %collective-permute-start.10 = (bf16[32,384]{1,0:T(8,128)(2,1)S(1)}, bf16[32,384]{1,0:T(8,128)(2,1)S(1)}, u32[]{:S(2)}, u32[]{:S(2)}) collective-permute-start(bf16[32,384]{1,0:T(8,128)(2,1)S(1)} %get-tuple-element.6), channel_id=1, source_target_pairs={{0,4},{4,8},{8,12},{1,5},{5,9},{9,13},{2,6},{6,10},{10,14},{3,7},{... | collective-permute-start | bytes 73736 | tf_op jit(solution)/shard_map/ppermute | solution.py:34
  61.8 1.0 fusion.31
  62.8 1.3 %collective-permute-start.9 = (bf16[32,384]{1,0:T(8,128)(2,1)S(1)}, bf16[32,384]{1,0:T(8,128)(2,1)S(1)}, u32[]{:S(2)}, u32[]{:S(2)}) collective-permute-start(bf16[32,384]{1,0:T(8,128)(2,1)S(1)} %get-tuple-element.5), channel_id=1, source_target_pairs={{4,0},{8,4},{12,8},{5,1},{9,5},{13,9},{6,2},{10,6},{14,10},{7,3},{... | collective-permute-start | bytes 73736 | tf_op jit(solution)/shard_map/ppermute | solution.py:36
  64.1 1.0 fusion.28
  65.1 3.4 %collective-permute-done.9 = bf16[32,384]{1,0:T(8,128)(2,1)S(1)} collective-permute-done((bf16[32,384]{1,0:T(8,128)(2,1)S(1)}, bf16[32,384]{1,0:T(8,128)(2,1)S(1)}, u32[]{:S(2)}, u32[]{:S(2)}) %collective-permute-start.9) | collective-permute-done | bytes 24608 | tf_op jit(solution)/shard_map/ppermute | solution.py:36
  68.5 2.7 %fusion.8 = f32[512,1536]{1,0:T(8,128)} fusion(f32[512,1536]{1,0:T(8,128)S(1)} %fusion.28, f32[512,1536]{1,0:T(8,128)S(1)} %fusion.31, bf16[3,1536,384]{2,1,0:T(8,128)(2,1)S(1)} %copy-done.1, bf16[32,384]{1,0:T(8,128)(2,1)S(1)} %collective-permute-done.9, bf16[512,384]{1,0:T(8,128)(2,1)S(1)} %multiply_convert_fusion), kind=kOutput, calls=%fused_computation.13 | convolution fusion | flops 606339072 | bytes 11034624 | tf_op jit(solution)/shard_map/dot_general | solution.py:128
  71.3 0.0 all-reduce.2.cloned.1.call-update
  71.3 0.7 copy-done.4
  71.9 20.4 %all-reduce.2.cloned.1.call-done = f32[512,1536]{1,0:T(8,128)} async-done(((f32[512,1536]{1,0:T(8,128)}), f32[512,1536]{1,0:T(8,128)}) %all-reduce.2.cloned.1.call-update) | async-done | bytes 3145744 | tf_op jit(solution)/shard_map/psum | solution.py:135
  92.3 4.1 %fusion.14 = f32[512,1536]{1,0:T(8,128)S(1)} fusion(f32[576,1536]{1,0:T(8,128)} %get-tuple-element.18, f32[512,1536]{1,0:T(8,128)} %all-reduce.2.cloned.1.call-done, f32[1536]{0:T(1024)S(1)} %convert_element_type.38), kind=kLoop, calls=%fused_computation.19 | loop fusion | flops 15728640 | bytes 9443328 | tf_op jit(solution)/shard_map/transpose(jvp())/add_any | solution.py:49
  96.4 0.6 fusion.15
  97.0 0.6 convolution_add_fusion.1
  97.6 0.4 fusion.59
  98.0 20.5 %all_to_all.21 = f32[8,32,512]{2,1,0:T(8,128)S(1)} all-to-all(f32[8,32,512]{2,1,0:T(8,128)S(1)} %fusion.59), channel_id=1, replica_groups=mesh['groups'=2,'locus'=4,'design'=2,'chan'=2] {'locus','design'}, dimensions={0} | all-to-all | bytes 1048576 | tf_op jit(solution)/shard_map/all_to_all | solution.py:141
  118.5 1.1 fusion.57
  (33 shorter events, 0.2 us)
Async XLA Ops:
  6.5 22.9 %copy-start = (bf16[384,1536]{1,0:T(8,128)(2,1)S(1)}, bf16[384,1536]{1,0:T(8,128)(2,1)}, u32[]{:S(2)}) copy-start(bf16[384,1536]{1,0:T(8,128)(2,1)} %param.14) | copy-start | bytes 3538948
  6.5 39.8 %copy-start.3 = (bf16[1,512,128]{2,1,0:T(8,128)(2,1)S(1)}, bf16[1,512,128]{2,1,0:T(8,128)(2,1)}, u32[]{:S(2)}) copy-start(bf16[1,512,128]{2,1,0:T(8,128)(2,1)} %param.8) | copy-start | bytes 393220
  6.5 42.5 %copy-start.2 = (bf16[128,768]{1,0:T(8,128)(2,1)S(1)}, bf16[128,768]{1,0:T(8,128)(2,1)}, u32[]{:S(2)}) copy-start(bf16[128,768]{1,0:T(8,128)(2,1)} %param.12) | copy-start | bytes 589828
  10.5 19.4 %all-to-all-start = ((s32[8,32,1]{1,2,0:T(1,128)}), s32[8,32,1]{1,2,0:T(1,128)S(1)}, u32[]{:S(2)}, u32[]{:S(2)}) async-start(s32[8,32,1]{1,2,0:T(1,128)} %all_to_all.14), calls=%async_computation | async-start | bytes 8192 | tf_op jit(solution)/shard_map/all_to_all | solution.py:98
  17.8 74.6 %all-reduce.2.cloned.1.call-start = ((), (), s32[]{:S(2)}) async-start(), calls=%async_computation.2 | async-start | bytes 6291456 | tf_op jit(solution)/shard_map/psum | solution.py:135
  19.1 26.3 %collective-permute-start.6 = (bf16[32,512]{1,0:T(8,128)(2,1)S(1)}, bf16[32,512]{1,0:T(8,128)(2,1)S(1)}, u32[]{:S(2)}, u32[]{:S(2)}) collective-permute-start(bf16[32,512]{1,0:T(8,128)(2,1)S(1)} %get-tuple-element.7), channel_id=1, source_target_pairs={{0,14},{2,0},{4,2},{6,4},{8,6},{10,8},{12,10},{14,12},{1,15},{3,1}... | collective-permute-start | bytes 98312 | tf_op jit(solution)/shard_map/ppermute | solution.py:73
  23.8 21.7 %collective-permute-start.5 = (bf16[32,512]{1,0:T(8,128)(2,1)S(1)}, bf16[32,512]{1,0:T(8,128)(2,1)S(1)}, u32[]{:S(2)}, u32[]{:S(2)}) collective-permute-start(bf16[32,512]{1,0:T(8,128)(2,1)S(1)} %get-tuple-element.8), channel_id=1, source_target_pairs={{0,12},{2,14},{4,0},{6,2},{8,4},{10,6},{12,8},{14,10},{1,13},{3,15... | collective-permute-start | bytes 98312 | tf_op jit(solution)/shard_map/ppermute | solution.py:73
  24.3 21.1 %collective-permute-start.4 = (bf16[32,512]{1,0:T(8,128)(2,1)S(1)}, bf16[32,512]{1,0:T(8,128)(2,1)S(1)}, u32[]{:S(2)}, u32[]{:S(2)}) collective-permute-start(bf16[32,512]{1,0:T(8,128)(2,1)S(1)} %get-tuple-element.9), channel_id=1, source_target_pairs={{0,10},{2,12},{4,14},{6,0},{8,2},{10,4},{12,6},{14,8},{1,11},{3,13... | collective-permute-start | bytes 98312 | tf_op jit(solution)/shard_map/ppermute | solution.py:73
  24.3 21.1 %collective-permute-start.3 = (bf16[32,512]{1,0:T(8,128)(2,1)S(1)}, bf16[32,512]{1,0:T(8,128)(2,1)S(1)}, u32[]{:S(2)}, u32[]{:S(2)}) collective-permute-start(bf16[32,512]{1,0:T(8,128)(2,1)S(1)} %get-tuple-element.10), channel_id=1, source_target_pairs={{0,8},{2,10},{4,12},{6,14},{8,0},{10,2},{12,4},{14,6},{1,9},{3,11}... | collective-permute-start | bytes 98312 | tf_op jit(solution)/shard_map/ppermute | solution.py:73
  27.2 6.7 %collective-permute-start = (bf16[32,512]{1,0:T(8,128)(2,1)S(1)}, bf16[32,512]{1,0:T(8,128)(2,1)S(1)}, u32[]{:S(2)}, u32[]{:S(2)}) collective-permute-start(bf16[32,512]{1,0:T(8,128)(2,1)S(1)} %get-tuple-element.13), channel_id=1, source_target_pairs={{0,2},{2,4},{4,6},{6,8},{8,10},{10,12},{12,14},{14,0},{1,3},{3,5},... | collective-permute-start | bytes 98312 | tf_op jit(solution)/shard_map/ppermute | solution.py:73
  34.0 5.7 %collective-permute-start.1 = (bf16[32,512]{1,0:T(8,128)(2,1)S(1)}, bf16[32,512]{1,0:T(8,128)(2,1)S(1)}, u32[]{:S(2)}, u32[]{:S(2)}) collective-permute-start(bf16[32,512]{1,0:T(8,128)(2,1)S(1)} %get-tuple-element.12), channel_id=1, source_target_pairs={{0,4},{2,6},{4,8},{6,10},{8,12},{10,14},{12,0},{14,2},{1,5},{3,7},... | collective-permute-start | bytes 98312 | tf_op jit(solution)/shard_map/ppermute | solution.py:73
  39.7 5.7 %collective-permute-start.2 = (bf16[32,512]{1,0:T(8,128)(2,1)S(1)}, bf16[32,512]{1,0:T(8,128)(2,1)S(1)}, u32[]{:S(2)}, u32[]{:S(2)}) collective-permute-start(bf16[32,512]{1,0:T(8,128)(2,1)S(1)} %get-tuple-element.11), channel_id=1, source_target_pairs={{0,6},{2,8},{4,10},{6,12},{8,14},{10,0},{12,2},{14,4},{1,7},{3,9},... | collective-permute-start | bytes 98312 | tf_op jit(solution)/shard_map/ppermute | solution.py:73
  46.4 4.7 %collective-permute-start.7 = (bf16[32,128]{1,0:T(8,128)(2,1)S(1)}, bf16[32,128]{1,0:T(8,128)(2,1)S(1)}, u32[]{:S(2)}, u32[]{:S(2)}) collective-permute-start(bf16[32,128]{1,0:T(8,128)(2,1)S(1)} %get-tuple-element.15), channel_id=1, source_target_pairs={{0,4},{4,8},{8,12},{1,5},{5,9},{9,13},{2,6},{6,10},{10,14},{3,7},{... | collective-permute-start | bytes 24584 | tf_op jit(solution)/shard_map/ppermute | solution.py:34
  47.7 5.5 %collective-permute-start.8 = (bf16[32,128]{1,0:T(8,128)(2,1)S(1)}, bf16[32,128]{1,0:T(8,128)(2,1)S(1)}, u32[]{:S(2)}, u32[]{:S(2)}) collective-permute-start(bf16[32,128]{1,0:T(8,128)(2,1)S(1)} %get-tuple-element.16), channel_id=1, source_target_pairs={{4,0},{8,4},{12,8},{5,1},{9,5},{13,9},{6,2},{10,6},{14,10},{7,3},{... | collective-permute-start | bytes 24584 | tf_op jit(solution)/shard_map/ppermute | solution.py:36
  51.1 5.1 %copy-start.1 = (bf16[3,1536,384]{2,1,0:T(8,128)(2,1)S(1)}, bf16[3,1536,384]{2,1,0:T(8,128)(2,1)}, u32[]{:S(2)}) copy-start(bf16[3,1536,384]{2,1,0:T(8,128)(2,1)} %param.13) | copy-start | bytes 10616836
  59.4 4.7 %collective-permute-start.10 = (bf16[32,384]{1,0:T(8,128)(2,1)S(1)}, bf16[32,384]{1,0:T(8,128)(2,1)S(1)}, u32[]{:S(2)}, u32[]{:S(2)}) collective-permute-start(bf16[32,384]{1,0:T(8,128)(2,1)S(1)} %get-tuple-element.6), channel_id=1, source_target_pairs={{0,4},{4,8},{8,12},{1,5},{5,9},{9,13},{2,6},{6,10},{10,14},{3,7},{... | collective-permute-start | bytes 73736 | tf_op jit(solution)/shard_map/ppermute | solution.py:34
  62.8 5.7 %collective-permute-start.9 = (bf16[32,384]{1,0:T(8,128)(2,1)S(1)}, bf16[32,384]{1,0:T(8,128)(2,1)S(1)}, u32[]{:S(2)}, u32[]{:S(2)}) collective-permute-start(bf16[32,384]{1,0:T(8,128)(2,1)S(1)} %get-tuple-element.5), channel_id=1, source_target_pairs={{4,0},{8,4},{12,8},{5,1},{9,5},{13,9},{6,2},{10,6},{14,10},{7,3},{... | collective-permute-start | bytes 73736 | tf_op jit(solution)/shard_map/ppermute | solution.py:36
  71.3 0.7 copy-start.4
Sparse Core Ops, SparseCore 0:
  71.4 20.8 all-reduce.1
